TPU v7x, 32 devices: a whole 2x2x4 slice. The times are simulated.
32 devices in a mesh: replica: 8 (over y, x, core), fsdp: 4 (over z).
Axes of the slice: x: 2, y: 2, z: 4, core: 2. Of those that a mesh axis runs over, the one named last changes fastest.
Arguments:
- tokens: bfloat16 [4096, 8192], P(('replica', 'fsdp')), may hold values from -6 to 6
- weight: bfloat16 [192, 8192], P(None, 'fsdp'), may hold values from -0.0625 to 0.0625
- cotangent: bfloat16 [4096, 192], P(('replica', 'fsdp')), may hold values from -0.119628906 to 0.119628906
- momentum: float32 [8, 192, 8192], P('replica', None, 'fsdp'), may hold values from -6 to 6
- chosen: int32 [8, 3, 128, 32], P('replica', None, 'fsdp'), may hold values from 0 to 4095, as said below
Outputs:
- new_momentum: float32 [8, 192, 8192], P('replica', None, 'fsdp')
- update: float32 [192, 8192], P(None, 'fsdp')
Inputs may be any that keep to these rules, and one draw needn't show every extreme that they name: `chosen`: within each block the 32 positions are distinct; the block's 64 * 64 positions fall into 32 equal runs of consecutive positions and each run holds exactly one of them.
All inputs are finite; a program needn't handle non-finite values.
Results may differ from a plain program's by a relative error of at most 0.003.
Values may be sent and summed in bfloat16 or wider, within the bound.
A program may use at most 64 MiB of HBM per device.

v0:
```python
import math

import jax
import jax.numpy as jnp
from jax import lax
from jax.sharding import PartitionSpec as P

SPAN = 64
TOPK = 32


decay = 0.999


def cosine_table():
    points = jnp.arange(SPAN, dtype=jnp.float32)
    angles = math.pi * (2.0 * points[None, :] + 1.0) * points[:, None] / (2.0 * SPAN)
    scales = jnp.where(points[:, None] == 0, math.sqrt(1.0 / SPAN), math.sqrt(2.0 / SPAN))
    return scales * jnp.cos(angles)


def forward_dct(moment, cosines):
    blocks_a = moment.shape[0] // SPAN
    blocks_b = moment.shape[1] // SPAN
    tiles = moment.reshape(blocks_a, SPAN, blocks_b, SPAN)
    coefficients = jnp.einsum(
        "ki,aibj,lj->abkl", cosines, tiles, cosines, precision=lax.Precision.HIGHEST
    )
    return coefficients.reshape(blocks_a, blocks_b, SPAN * SPAN)


def inverse_dct(spread, cosines):
    blocks_a = spread.shape[0]
    blocks_b = spread.shape[1]
    tiles = spread.reshape(blocks_a, blocks_b, SPAN, SPAN)
    moment = jnp.einsum(
        "ki,abkl,lj->aibj", cosines, tiles, cosines, precision=lax.Precision.HIGHEST
    )
    return moment.reshape(blocks_a * SPAN, blocks_b * SPAN)


def run_masks(positions):
    run_length = SPAN * SPAN // TOPK
    starts = jnp.arange(TOPK, dtype=jnp.int32) * run_length
    offsets = positions - starts
    slots = jnp.arange(run_length, dtype=jnp.int32)
    return offsets[..., None] == slots


def gate_gradient(preact, cotangent):
    sigmoid_value = jax.nn.sigmoid(preact)
    return (
        cotangent.astype(jnp.float32) * sigmoid_value * (1.0 + preact * (1.0 - sigmoid_value))
    ).astype(jnp.bfloat16)


def shards(tokens, weight, cotangent, momentum, chosen):
    cosines = cosine_table()
    columns = tokens
    preact = lax.dot_general(
        columns,
        lax.all_gather(weight, "fsdp", axis=1, tiled=True),
        (((1,), (1,)), ((), ())),
        preferred_element_type=jnp.float32,
    )
    gate_grad = gate_gradient(preact, cotangent)
    columns = tokens
    gradient = (
        lax.psum_scatter(
            lax.dot_general(
                columns, gate_grad, (((0,), (0,)), ((), ())), preferred_element_type=jnp.float32
            ).astype(jnp.bfloat16),
            "fsdp",
            scatter_dimension=0,
            tiled=True,
        )
        .astype(jnp.float32)
        .T
    )
    moment = decay * momentum[0] + gradient
    coefficients = forward_dct(moment, cosines)
    blocks_a = coefficients.shape[0]
    blocks_b = coefficients.shape[1]
    run_length = SPAN * SPAN // TOPK
    runs = coefficients.reshape(blocks_a, blocks_b, TOPK, run_length)
    positions = chosen[0]
    masks = run_masks(positions)
    picked = jnp.sum(jnp.where(masks, runs, 0.0), axis=3)
    own = jnp.where(masks, picked[..., None], 0.0).reshape(blocks_a, blocks_b, SPAN * SPAN)
    new_moment = moment - inverse_dct(own, cosines)
    values, all_positions = (
        lax.all_gather(picked[None], "replica", axis=0, tiled=True),
        lax.all_gather(chosen, "replica", axis=0, tiled=True),
    )
    members = values.shape[0]
    group = math.gcd(members, 8)

    def add_group(turn, total):
        value_part = lax.dynamic_slice_in_dim(values, turn * group, group, 0)
        position_part = lax.dynamic_slice_in_dim(all_positions, turn * group, group, 0)
        placed = jnp.where(run_masks(position_part), value_part[..., None], 0.0)
        return total + jnp.sum(placed, axis=0)

    start_total = jnp.zeros((blocks_a, blocks_b, TOPK, run_length), jnp.float32)
    spread = lax.fori_loop(0, members // group, add_group, start_total).reshape(
        blocks_a, blocks_b, SPAN * SPAN
    )
    update = inverse_dct(spread, cosines)
    return (new_moment[None], update)


def solution(mesh):
    return jax.shard_map(
        shards,
        mesh=mesh,
        in_specs=(
            P(("replica", "fsdp"), None),
            P(None, "fsdp"),
            P(("replica", "fsdp"), None),
            P("replica", None, "fsdp"),
            P("replica", None, "fsdp", None),
        ),
        out_specs=(P("replica", None, "fsdp"), P(None, "fsdp")),
        check_vma=False,
    )
```

profile of v0, /device:TPU:0, one launch (start us, length us, event | category | flops | bytes accessed | tf_op | source)
XLA Modules:
  0.0 229.4 jit_solution(13701755142013738066)
XLA Ops:
  7.2 0.0 copy-start
  7.2 0.0 all-gather.3.cloned.1.call-start
  7.2 0.7 all-gather.3.cloned.1.call-update
  7.9 0.0 reduce-scatter.2.cloned.1.call-start
  8.0 67.8 %all-gather.3.cloned.1.call-done = bf16[192,8192]{1,0:T(8,128)(2,1)} async-done(((bf16[192,2048]{1,0:T(8,128)(2,1)}), bf16[192,8192]{1,0:T(8,128)(2,1)}) %all-gather.3.cloned.1.call-update) | async-done | bytes 3145744 | tf_op jit(solution)/shard_map/all_gather | solution.py:62
  75.8 0.0 copy-done
  75.8 7.1 %fusion = bf16[8192,192]{0,1:T(8,128)(2,1)} fusion(bf16[128,8192]{1,0:T(8,128)(2,1)S(1)} %copy-done, bf16[128,192]{0,1:T(8,128)(2,1)} %param.7, bf16[192,8192]{1,0:T(8,128)(2,1)} %all-gather.3.cloned.1.call-done), kind=kOutput, calls=%fused_computation.3 | convolution fusion | flops 807124992 | bytes 8437760 | tf_op jit(solution)/shard_map/dot_general | solution.py:70
  82.8 0.0 copy-start.1
  82.8 0.0 reduce-scatter.2.cloned.1.call-update
  82.9 0.1 copy.52
  83.0 0.7 copy-done.1
  83.6 0.1 copy.50
  83.8 0.1 copy.51
  83.8 9.5 %all_gather.10 = s32[8,3,32,32]{3,2,1,0:T(8,128)S(1)} all-gather(s32[1,3,32,32]{3,2,1,0:T(8,128)S(1)} %copy-done.1), channel_id=1, replica_groups=mesh['replica'=8,'fsdp'=4] {'replica'}, dimensions={0}, use_global_device_ids=true | all-gather | bytes 110592 | tf_op jit(solution)/shard_map/all_gather | solution.py:93
  93.4 48.5 %reduce-scatter.2.cloned.1.call-done = bf16[2048,192]{0,1:T(8,128)(2,1)} async-done(((bf16[8192,192]{0,1:T(8,128)(2,1)}), bf16[2048,192]{0,1:T(8,128)(2,1)}) %reduce-scatter.2.cloned.1.call-update) | async-done | bytes 786448 | tf_op jit(solution)/shard_map/reduce_scatter | solution.py:69
  142.0 3.1 %bitcast_add_fusion = f32[192,2048]{1,0:T(8,128)} fusion(bf16[2048,192]{0,1:T(8,128)(2,1)} %reduce-scatter.2.cloned.1.call-done, f32[1,192,2048]{2,1,0:T(8,128)} %param.8), kind=kLoop, calls=%fused_computation.12 | loop fusion | flops 1179648 | bytes 3932160 | tf_op jit(solution)/shard_map/add | solution.py:80
  145.0 3.8 %reshape.57 = f32[3,64,32,64]{3,2,1,0:T(8,128)} reshape(f32[192,2048]{1,0:T(8,128)} %bitcast_add_fusion) | data formatting | bytes 3145728 | tf_op jit(solution)/shard_map/reshape | solution.py:25
  148.8 8.3 %fusion.3 = f32[3,32,64,64]{3,2,1,0:T(8,128)S(1)} fusion(f32[3,64,32,64]{3,2,1,0:T(8,128)} %reshape.57, f32[64]{0:T(128)S(1)} %get-tuple-element.13, f32[64]{0:T(128)S(1)} %get-tuple-element.12), kind=kOutput, calls=%fused_computation.8 | convolution fusion | flops 302002176 | bytes 3146240 | tf_op jit(solution)/shard_map/ki,aibj,lj->abkl/dot_general | solution.py:26
  157.1 3.6 %fusion.1 = f32[3,32,64]{2,1,0:T(8,128)S(1)} fusion(f32[3,32,64,64]{3,2,1,0:T(8,128)S(1)} %fusion.3, s32[64,64]{0,1:T(8,128)S(1)} %copy.52, s32[3,32,64]{2,1,0:T(8,128)S(1)} %copy.51, f32[64]{0:T(128)S(1)} %get-tuple-element.13, f32[64]{0:T(128)S(1)} %get-tuple-element.12), kind=kOutput, calls=%fused_computation.6 | convolution fusion | flops 303175680 | bytes 1638912 | tf_op jit(solution)/shard_map/ki,aibj,lj->abkl/dot_general | solution.py:26
  160.7 0.1 copy.54
  160.8 0.1 reduce_sum.28
  160.9 0.1 copy.58
  161.1 0.1 copy.55
  161.2 9.4 %fusion.2 = f32[3,32,64,64]{2,3,1,0:T(8,128)S(1)} fusion(f32[3,32,64]{2,1,0:T(8,128)S(1)} %copy.55, s32[64,64]{0,1:T(8,128)S(1)} %copy.52, s32[3,32,64]{2,1,0:T(8,128)S(1)} %copy.51, f32[64]{0:T(128)S(1)} %get-tuple-element.13, f32[64]{0:T(128)S(1)} %get-tuple-element.12), kind=kOutput, calls=%fused_computation.7 | convolution fusion | flops 302788608 | bytes 1638912 | tf_op jit(solution)/shard_map/ki,abkl,lj->aibj/dot_general | solution.py:36
  170.6 2.9 %convolution_bitcast_fusion.1 = f32[3,64,32,64]{3,1,2,0:T(8,128)S(1)} fusion(f32[3,32,64,64]{2,3,1,0:T(8,128)S(1)} %fusion.2, f32[64]{0:T(128)S(1)} %get-tuple-element.13, f32[64]{0:T(128)S(1)} %get-tuple-element.12), kind=kOutput, calls=%fused_computation.11 | convolution fusion | flops 302002176 | bytes 3146240 | tf_op jit(solution)/shard_map/ki,abkl,lj->aibj/dot_general | solution.py:36
  173.5 3.5 %copy.57 = f32[3,64,32,64]{3,2,1,0:T(8,128)} copy(f32[3,64,32,64]{3,1,2,0:T(8,128)S(1)} %convolution_bitcast_fusion.1) | data formatting | bytes 3145728 | tf_op jit(solution)/shard_map/ki,abkl,lj->aibj/transpose | solution.py:36
  177.0 3.8 %reshape.58 = f32[192,2048]{1,0:T(8,128)} reshape(f32[3,64,32,64]{3,2,1,0:T(8,128)} %copy.57) | data formatting | bytes 3145728 | tf_op jit(solution)/shard_map/reshape | solution.py:39
  180.7 3.2 %subtract_bitcast_fusion = f32[1,192,2048]{2,1,0:T(8,128)} fusion(f32[192,2048]{1,0:T(8,128)} %bitcast_add_fusion, f32[192,2048]{1,0:T(8,128)} %reshape.58), kind=kLoop, calls=%fused_computation.13 | loop fusion | flops 393216 | bytes 4718592 | tf_op jit(solution)/shard_map/broadcast_in_dim | solution.py:109
  184.0 9.5 %all-gather = f32[24,32,32]{2,1,0:T(8,128)S(1)} all-gather(f32[3,32,32]{2,1,0:T(8,128)S(1)} %copy.58), channel_id=2, replica_groups=mesh['replica'=8,'fsdp'=4] {'replica'}, dimensions={0}, use_global_device_ids=true | all-gather | bytes 110592 | tf_op jit(solution)/shard_map/all_gather | solution.py:92
  193.5 10.0 %select_reduce_fusion = f32[3,32,32,128]{3,2,1,0:T(8,128)} fusion(f32[8,3,32,32]{3,2,1,0:T(8,128)S(1)} %bitcast.47, s32[8,3,32,32]{3,2,1,0:T(8,128)S(1)} %broadcast_subtract_fusion), kind=kLoop, calls=%fused_computation | loop fusion | flops 9043968 | bytes 1769472 | tf_op jit(solution)/shard_map/while/body/eval_jaxpr/reduce_sum | solution.py:102
  203.5 3.3 %reshape_reshape.2 = f32[3,32,64,64]{3,2,1,0:T(8,128)} reshape(f32[3,32,32,128]{3,2,1,0:T(8,128)} %select_reduce_fusion) | data formatting | bytes 3145728 | tf_op jit(solution)/shard_map/reshape;reshape | solution.py:35
  206.9 5.0 %fusion.11 = f32[3,32,64,64]{2,3,1,0:T(8,128)S(1)} fusion(f32[3,32,64,64]{3,2,1,0:T(8,128)} %reshape_reshape.2, f32[64]{0:T(128)S(1)} %get-tuple-element.13, f32[64]{0:T(128)S(1)} %get-tuple-element.12), kind=kOutput, calls=%fused_computation.23 | convolution fusion | flops 302002176 | bytes 3146240 | tf_op jit(solution)/shard_map/ki,abkl,lj->aibj/dot_general | solution.py:36
  211.9 2.9 %convolution_bitcast_fusion = f32[3,64,32,64]{3,1,2,0:T(8,128)S(1)} fusion(f32[3,32,64,64]{2,3,1,0:T(8,128)S(1)} %fusion.11, f32[64]{0:T(128)S(1)} %get-tuple-element.13, f32[64]{0:T(128)S(1)} %get-tuple-element.12), kind=kOutput, calls=%fused_computation.10 | convolution fusion | flops 302002176 | bytes 3146240 | tf_op jit(solution)/shard_map/ki,abkl,lj->aibj/dot_general | solution.py:36
  214.8 3.5 %copy.61 = f32[3,64,32,64]{3,2,1,0:T(8,128)} copy(f32[3,64,32,64]{3,1,2,0:T(8,128)S(1)} %convolution_bitcast_fusion) | data formatting | bytes 3145728 | tf_op jit(solution)/shard_map/ki,abkl,lj->aibj/transpose | solution.py:36
  218.3 3.8 %reshape.59 = f32[192,2048]{1,0:T(8,128)} reshape(f32[3,64,32,64]{3,2,1,0:T(8,128)} %copy.61) | data formatting | bytes 3145728 | tf_op jit(solution)/shard_map/reshape | solution.py:39
  (8 shorter events, 0.1 us)
Async XLA Ops:
  7.2 68.6 %copy-start = (bf16[128,8192]{1,0:T(8,128)(2,1)S(1)}, bf16[128,8192]{1,0:T(8,128)(2,1)}, u32[]{:S(2)}) copy-start(bf16[128,8192]{1,0:T(8,128)(2,1)} %param.5) | copy-start | bytes 6291460
  7.2 68.6 %all-gather.3.cloned.1.call-start = ((), (), s32[]{:S(2)}) async-start(), calls=%async_computation.1 | async-start | bytes 3932160 | tf_op jit(solution)/shard_map/all_gather | solution.py:62
  7.9 134.0 %reduce-scatter.2.cloned.1.call-start = ((), (), s32[]{:S(2)}) async-start(), calls=%async_computation.2 | async-start | bytes 3932160 | tf_op jit(solution)/shard_map/reduce_scatter | solution.py:69
  82.8 0.8 copy-start.1
Sparse Core Ops, SparseCore 0:
  9.6 66.1 all-gather.2
  83.0 58.9 reduce-scatter.1
where the time goes:
time: 234 us; the launch traced here: 229 us
  waiting for transfers between devices  117 us (50%)
  matrix products  39.2 us (17%)
  local copies, waits for them, and re-layouts  22.8 us (10%)
  blocking collectives  19.1 us (8%)
  other arithmetic  16.5 us (7%)
  between operations  14.6 us (6%)
    all_gather x1, waiting for transfers between devices, shards(): lax.all_gather(weight, 'fsdp', axis=1, tiled=True)  67.8 us
    reduce_scatter x1, waiting for transfers between devices, shards(): lax.psum_scatter(lax.dot_general(columns, gate_grad, (((0,), (0,)), ((),...  48.5 us
    dot_general x4, matrix products, inverse_dct(): jnp.einsum('ki,abkl,lj->aibj', cosines, tiles, cosines, precision=lax.Pre...  20.3 us
    dot_general x2, matrix products, forward_dct(): jnp.einsum('ki,aibj,lj->abkl', cosines, tiles, cosines, precision=lax.Pre...  11.9 us
    reduce_sum x1, other arithmetic, add_group(): return total + jnp.sum(placed, axis=0)  10 us
    all_gather x1, blocking collectives, shards(): lax.all_gather(chosen, 'replica', axis=0, tiled=True)  9.55 us
    all_gather x1, blocking collectives, shards(): lax.all_gather(picked[None], 'replica', axis=0, tiled=True)  9.54 us
    reshape x2, local copies, waits for them, and re-layouts, inverse_dct(): return moment.reshape(blocks_a * SPAN, blocks_b * SPAN)  7.52 us
  transfers between devices with their start and end apart: 2, of which 2 were waited for; matrix products, arithmetic and copies ran while one was open for 0% of the time, Pallas kernels for 0%

commit v1 on v0

v1 whole, which is shorter than its diff:
```python
import functools
import math

import jax
import jax.numpy as jnp
import ml_dtypes
import numpy as np
from jax import lax
from jax.experimental import pallas as pl
from jax.experimental.pallas import tpu as pltpu
from jax.sharding import PartitionSpec as P

SPAN = 64
TOPK = 32
RUN = SPAN * SPAN // TOPK
CHUNK = 512
GROUP = 8
decay = 0.999

BF = jnp.bfloat16
F32 = jnp.float32
MESH = pl.DeviceIdType.MESH


def cosine_table():
    n = np.arange(SPAN, dtype=np.float64)
    angles = math.pi * (2.0 * n[None, :] + 1.0) * n[:, None] / (2.0 * SPAN)
    scales = np.where(n[:, None] == 0, math.sqrt(1.0 / SPAN), math.sqrt(2.0 / SPAN))
    return (scales * np.cos(angles)).astype(np.float32)


def halves(table):
    high = table.astype(ml_dtypes.bfloat16)
    low = (table - high.astype(np.float32)).astype(ml_dtypes.bfloat16)
    return high, low


def split(x):
    high = x.astype(BF)
    return high, (x - high.astype(F32)).astype(BF)


def mm(a, b):
    return jnp.dot(a, b, preferred_element_type=F32)


def mm_nt(a, b):
    return lax.dot_general(a, b, (((1,), (1,)), ((), ())), preferred_element_type=F32)


def transform(x, left_high, left_low, right_high, right_low):
    high, low = split(x)
    half = mm(left_high, high) + mm(left_high, low) + mm(left_low, high)
    width = right_high.shape[0]
    parts = []
    for start in range(0, x.shape[1], width):
        high, low = split(half[:, start : start + width])
        parts.append(mm(high, right_high) + mm(high, right_low) + mm(low, right_high))
    return jnp.concatenate(parts, axis=1)


def kernel(
    nf, nr,
    tok, weight, cot, mom, chosen,
    fwd_lh, fwd_ll, fwd_rh, fwd_rl, inv_lh, inv_ll, inv_rh, inv_rl, eye, pair, wide, spot, wide8,
    new_out, upd_out,
    tok_v, w_own, wall, cot_v, mom_v, xall, gt, pos, delta, vt, new_v, upd_v,
    s1_s, s1_r, s2_s, s2_r, s3_s, s3_r, x_s, x_r, g_s, g_r, p_s, p_r, v_s, v_r, loc, xloc, osem,
):
    r, f = lax.axis_index("replica"), lax.axis_index("fsdp")
    rows, dc = weight.shape
    td = tok.shape[0]
    nch = dc // CHUNK
    half = dc // 2
    inner = lax.rem(r, 8)
    base = r - inner
    quad, side = inner // 2, lax.rem(inner, 2)
    piece = rows // 4

    def fpeer(k):
        return lax.rem(f + k, nf)

    def fsource(k):
        return lax.rem(f + nf - k, nf)

    def remote(src, dst, send, recv, to_r, to_f):
        return pltpu.make_async_remote_copy(
            src_ref=src, dst_ref=dst, send_sem=send, recv_sem=recv,
            device_id=(to_r, to_f), device_id_type=MESH,
        )

    c_tok = pltpu.make_async_copy(tok, tok_v, loc.at[0])
    c_w = pltpu.make_async_copy(weight, w_own, loc.at[1])
    c_cot = pltpu.make_async_copy(cot, cot_v, loc.at[2])
    c_mom = pltpu.make_async_copy(mom.at[0], mom_v, loc.at[3])
    c_pos = pltpu.make_async_copy(chosen.at[0], pos.at[r], loc.at[4])
    c_x = [
        pltpu.make_async_copy(
            tok.at[:, pl.ds(pl.multiple_of(f * dc + c * CHUNK, CHUNK), CHUNK)],
            xall.at[c, pl.ds(pl.multiple_of(f * td, td), td)],
            xloc.at[c],
        )
        for c in range(nch)
    ]
    for copy in [c_w, c_tok, c_pos, c_cot, c_mom] + c_x:
        copy.start()

    barrier = pltpu.get_barrier_semaphore()
    for k in range(1, nf):
        pl.semaphore_signal(barrier, inc=1, device_id=(r, fpeer(k)), device_id_type=MESH)
    for t in range(1, nr):
        pl.semaphore_signal(
            barrier, inc=1, device_id=(lax.rem(r + t, nr), f), device_id_type=MESH
        )
    pl.semaphore_wait(barrier, nf - 1 + nr - 1)

    own_rows = pl.ds(pl.multiple_of(quad * piece, 16), piece)
    stage1 = {}
    for k in range(1, nf):
        stage1[k] = remote(
            weight.at[own_rows, pl.ds(pl.multiple_of(side * half, half), half)],
            wall.at[f, side, own_rows],
            s1_s.at[k], s1_r.at[k], r, fpeer(k),
        )
        stage1[k].start()
    sent_pos = {}
    for t in range(1, nr):
        sent_pos[t] = remote(
            chosen.at[0], pos.at[r], p_s.at[t], p_r.at[t], lax.rem(r + t, nr), f
        )
        sent_pos[t].start()

    xs = {}

    def send_x(c):
        for k in range(1, nf):
            to = fpeer(k)
            xs[c, k] = remote(
                tok.at[:, pl.ds(pl.multiple_of(to * dc + c * CHUNK, CHUNK), CHUNK)],
                xall.at[c, pl.ds(pl.multiple_of(f * td, td), td)],
                x_s.at[k, c], x_r.at[k, c], r, to,
            )
            xs[c, k].start()

    c_tok.wait()
    c_w.wait()
    pre = mm_nt(w_own[...], tok_v[:, pl.ds(pl.multiple_of(f * dc, CHUNK), dc)])

    for k in range(1, nf):
        stage1[k].wait_send()
    send_x(0)

    stage2 = {}
    for k in range(1, nf):
        stage1[k].wait_recv()
        for t in range(1, 4):
            block = wall.at[fsource(k), side, own_rows]
            stage2[k, t] = remote(
                block, block, s2_s.at[k, t], s2_r.at[k, t],
                base + lax.rem(quad + t, 4) * 2 + side, f,
            )
            stage2[k, t].start()
    if nch > 1:
        send_x(1)

    c_pos.wait()
    for t in range(1, nr):
        sent_pos[t].wait_recv()
    row = lax.broadcasted_iota(jnp.int32, (rows, CHUNK), 0)
    col = lax.broadcasted_iota(jnp.int32, (rows, CHUNK), 1)
    target = (lax.rem(row, 2) * SPAN + lax.rem(col, SPAN)).astype(F32)
    run_start = lax.broadcasted_iota(jnp.int32, pos.shape[2:], 1) * RUN

    def locate(i, carry):
        parts = []
        for a in range(rows // SPAN):
            offset = (pos[i, a] - run_start).astype(F32).astype(BF)
            parts.append(mm_nt(pair[...], offset))
        spots = jnp.concatenate(parts, axis=0).astype(BF)
        for c in range(nch):
            far = mm(spots, wide[:, c * CHUNK : (c + 1) * CHUNK])
            delta[c, i] = (far - target).astype(BF)
        return carry

    def locate_some(low, high):
        lax.fori_loop(low, high, locate, 0)

    locate_some(0, nr // 2)

    stage3 = {}
    for k in range(1, nf):
        for t in range(1, 4):
            stage2[k, t].wait_recv()
        block = wall.at[fsource(k), side]
        stage3[k] = remote(block, block, s3_s.at[k], s3_r.at[k], r + 1 - 2 * side, f)
        stage3[k].start()
    for k in range(1, nf):
        stage3[k].wait_recv()
        source = fsource(k)
        for h in range(2):
            cols = pl.ds(pl.multiple_of(source * dc + h * half, 128), half)
            pre = pre + mm_nt(wall[source, h], tok_v[:, cols])

    c_cot.wait()
    up = mm_nt(eye[...], cot_v[...])
    s = jax.nn.sigmoid(pre)
    mine = pl.ds(pl.multiple_of(f * td, td), td)
    gt[:, mine] = (up * s * (1.0 + pre * (1.0 - s))).astype(BF)
    sent_g = {}
    for k in range(1, nf):
        sent_g[k] = remote(
            gt.at[:, mine], gt.at[:, mine], g_s.at[k], g_r.at[k], r, fpeer(k)
        )
        sent_g[k].start()

    def wait_x_sent(c):
        for k in range(1, nf):
            xs[c, k].wait_send()

    for c in range(2, nch):
        if c == 2:
            wait_x_sent(0)
            send_x(c)
    locate_some(nr // 2, nr)
    for k in range(1, nf):
        sent_g[k].wait_recv()
    c_mom.wait()

    sent_v = {}
    outs = []

    def first_half(c):
        c_x[c].wait()
        for k in range(1, nf):
            xs[c, k].wait_recv()
        cols = slice(c * CHUNK, (c + 1) * CHUNK)
        moment = decay * mom_v[:, cols] + mm(gt[...], xall[c])
        coef = transform(moment, fwd_lh[...], fwd_ll[...], fwd_rh[...], fwd_rl[...])
        own = jnp.where(delta[c, r].astype(F32) == 0.0, coef, 0.0)
        high, low = split(own)
        nbc = CHUNK // SPAN
        vt[c, r] = (mm_nt(spot[...], high) + mm_nt(spot[...], low))[:nbc]
        for t in range(1, nr):
            sent_v[c, t] = remote(
                vt.at[c, r], vt.at[c, r], v_s.at[c, t], v_r.at[c, t], lax.rem(r + t, nr), f
            )
            sent_v[c, t].start()
        new_v[:, cols] = moment - transform(
            own, inv_lh[...], inv_ll[...], inv_rh[...], inv_rl[...]
        )
        copy = pltpu.make_async_copy(new_v.at[:, cols], new_out.at[0, :, cols], osem.at[0, c])
        copy.start()
        outs.append(copy)

    def second_half(c):
        for t in range(1, nr):
            sent_v[c, t].wait_recv()
        cols = slice(c * CHUNK, (c + 1) * CHUNK)
        nbc = CHUNK // SPAN

        def add_group(g, total):
            first = pl.multiple_of(g * GROUP, GROUP)
            high, low = split(vt[c, pl.ds(first, GROUP)].reshape(GROUP * nbc, rows))
            both = mm_nt(eye[...], jnp.concatenate([high, low], axis=0)).astype(BF)
            for i in range(GROUP):
                value = mm(both, wide8[i])
                total = total + jnp.where(delta[c, first + i].astype(F32) == 0.0, value, 0.0)
            return total

        total = jnp.zeros((rows, CHUNK), F32)
        if nr == GROUP:
            total = add_group(0, total)
        else:
            total = lax.fori_loop(0, nr // GROUP, add_group, total)
        upd_v[:, cols] = transform(total, inv_lh[...], inv_ll[...], inv_rh[...], inv_rl[...])
        copy = pltpu.make_async_copy(upd_v.at[:, cols], upd_out.at[:, cols], osem.at[1, c])
        copy.start()
        outs.append(copy)

    for c in range(nch):
        first_half(c)
        if c + 3 < nch:
            wait_x_sent(c + 1)
            send_x(c + 3)
        if c > 0:
            second_half(c - 1)
    second_half(nch - 1)

    for c in range(max(nch - 2, 0), nch):
        wait_x_sent(c)
    for k in range(1, nf):
        for t in range(1, 4):
            stage2[k, t].wait_send()
        stage3[k].wait_send()
        sent_g[k].wait_send()
    for t in range(1, nr):
        sent_pos[t].wait_send()
        for c in range(nch):
            sent_v[c, t].wait_send()
    for copy in outs:
        copy.wait()


def shards(nf, nr, tokens, weight, cotangent, momentum, chosen):
    td = tokens.shape[0]
    rows, dc = weight.shape
    nb = dc // SPAN
    nch = dc // CHUNK
    nbc = CHUNK // SPAN
    table = cosine_table()
    left = np.kron(np.eye(rows // SPAN, dtype=np.float32), table)
    right = np.kron(np.eye(4, dtype=np.float32), table)
    fwd_lh, fwd_ll = halves(left)
    fwd_rh, fwd_rl = halves(np.ascontiguousarray(right.T))
    inv_lh, inv_ll = halves(np.ascontiguousarray(left.T))
    inv_rh, inv_rl = halves(right)
    bf = ml_dtypes.bfloat16
    eye = np.eye(rows, dtype=np.float32).astype(bf)
    pair = (np.arange(SPAN)[:, None] // 2 == np.arange(TOPK)[None, :]).astype(bf)
    wide = (np.arange(dc)[None, :] // SPAN == np.arange(nb)[:, None]).astype(bf)
    spot = (np.arange(CHUNK)[None, :] // SPAN == np.arange(2 * nbc)[:, None]).astype(bf)
    slot = np.arange(2 * GROUP * nbc) % (GROUP * nbc)
    wide8 = (
        (slot[None, :, None] // nbc == np.arange(GROUP)[:, None, None])
        & (slot[None, :, None] % nbc == np.arange(CHUNK)[None, None, :] // SPAN)
    ).astype(bf)
    consts = (
        fwd_lh, fwd_ll, fwd_rh, fwd_rl, inv_lh, inv_ll, inv_rh, inv_rl, eye, pair, wide, spot, wide8
    )
    dma = pltpu.SemaphoreType.DMA
    vm = pltpu.VMEM
    new, update = pl.pallas_call(
        functools.partial(kernel, nf, nr),
        out_shape=(
            jax.ShapeDtypeStruct((1, rows, dc), F32),
            jax.ShapeDtypeStruct((rows, dc), F32),
        ),
        in_specs=[pl.BlockSpec(memory_space=pl.ANY)] * 5
        + [pl.BlockSpec(memory_space=pltpu.VMEM)] * len(consts),
        out_specs=(pl.BlockSpec(memory_space=pl.ANY), pl.BlockSpec(memory_space=pl.ANY)),
        scratch_shapes=[
            vm(tokens.shape, BF),
            vm(weight.shape, BF),
            vm((nf, 2, rows, dc // 2), BF),
            vm(cotangent.shape, BF),
            vm((rows, dc), F32),
            vm((nch, nf * td, CHUNK), BF),
            vm((rows, nf * td), BF),
            vm((nr,) + chosen.shape[1:], jnp.int32),
            vm((nch, nr, rows, CHUNK), BF),
            vm((nch, nr, nbc, rows), F32),
            vm((rows, dc), F32),
            vm((rows, dc), F32),
            dma((nf,)), dma((nf,)),
            dma((nf, 4)), dma((nf, 4)),
            dma((nf,)), dma((nf,)),
            dma((nf, nch)), dma((nf, nch)),
            dma((nf,)), dma((nf,)),
            dma((nr,)), dma((nr,)),
            dma((nch, nr)), dma((nch, nr)),
            dma((5,)), dma((nch,)), dma((2, nch)),
        ],
        compiler_params=pltpu.CompilerParams(
            collective_id=0, has_side_effects=True, vmem_limit_bytes=48 * 1024 * 1024
        ),
    )(tokens, weight, cotangent, momentum, chosen, *consts)
    return new, update


def solution(mesh):
    return jax.shard_map(
        functools.partial(shards, mesh.shape["fsdp"], mesh.shape["replica"]),
        mesh=mesh,
        in_specs=(
            P(("replica", "fsdp"), None),
            P(None, "fsdp"),
            P(("replica", "fsdp"), None),
            P("replica", None, "fsdp"),
            P("replica", None, "fsdp", None),
        ),
        out_specs=(P("replica", None, "fsdp"), P(None, "fsdp")),
        check_vma=False,
    )
```

time: 234 us -> 90.2 us (0.39); the launches traced: 229 us -> 89.5 us
  waiting for transfers between devices: 117 us -> 0 us
  Pallas kernels: 0 us -> 71.3 us
  matrix products: 39.2 us -> 0 us
  blocking collectives: 19.1 us -> 0 us
  other arithmetic: 16.5 us -> 0 us
  between operations: 14.6 us -> 0.68 us
  local copies, waits for them, and re-layouts: 22.8 us -> 17.6 us
    pallas_call x0 -> x1, Pallas kernels: none -> 71.3 us  [shards(): pl.pallas_call(functools.partial(kernel, nf, nr), out_shape=(jax.ShapeDty...]
    all_gather x1 -> x0, waiting for transfers between devices: 67.8 us -> none  [shards(): lax.all_gather(weight, 'fsdp', axis=1, tiled=True)]
    reduce_scatter x1 -> x0, waiting for transfers between devices: 48.5 us -> none  [shards(): lax.psum_scatter(lax.dot_general(columns, gate_grad, (((0,), (0,)), ((),...]
    dot_general x7 -> x0, matrix products: 39.2 us -> none  [the longest x4 20.3 us: inverse_dct(): jnp.einsum('ki,abkl,lj->aibj', cosines, tiles, cosines, precision=lax.Pre...]
    all_gather x2 -> x0, blocking collectives: 19.1 us -> none  [the longest x1 9.55 us: shards(): lax.all_gather(chosen, 'replica', axis=0, tiled=True)]
    unnamed x4 -> x35, local copies, waits for them, and re-layouts: 0.67 us -> 17.6 us
    reshape x3 -> x0, local copies, waits for them, and re-layouts: 11.3 us -> none  [the longest x2 7.52 us: inverse_dct(): return moment.reshape(blocks_a * SPAN, blocks_b * SPAN)]
    reduce_sum x2 -> x0, other arithmetic: 10.1 us -> none  [the longest x1 10 us: add_group(): return total + jnp.sum(placed, axis=0)]
  transfers between devices with their start and end apart: 2 -> 0, of which waited for: 2 -> 0; matrix products, arithmetic and copies ran while one was open for 0% -> 0% of each run, Pallas kernels for 0% -> 0%
where the time goes in v1:
time: 90.2 us; the launch traced here: 89.5 us
  Pallas kernels  71.3 us (79%)
  local copies, waits for them, and re-layouts  17.6 us (20%)
    pallas_call x1, Pallas kernels, shards(): pl.pallas_call(functools.partial(kernel, nf, nr), out_shape=(jax.ShapeDty...  71.3 us
    unnamed x35, local copies, waits for them, and re-layouts  17.6 us

profile of v1, /device:TPU:0, one launch (start us, length us, event | category | flops | bytes accessed | tf_op | source)
XLA Modules:
  0.0 89.5 jit_solution(6956216457084091328)
XLA Ops:
  0.6 0.9 %copy.20.cot = bf16[128,192]{1,0:T(8,128)(2,1)S(1)} copy(bf16[128,192]{0,1:T(8,128)(2,1)} %param.20) | data formatting | bytes 98304 | tf_op args[2]
  1.5 0.0 copy-start
  1.5 1.2 %copy-done = bf16[8,128,512]{2,1,0:T(8,128)(2,1)S(1)} copy-done((bf16[8,128,512]{2,1,0:T(8,128)(2,1)S(1)}, bf16[8,128,512]{2,1,0:T(8,128)(2,1)}, u32[]{:S(2)}) %copy-start) | copy-done | bytes 1048600
  2.8 0.0 copy-start.1
  2.8 1.1 %copy-done.1 = bf16[192,2048]{1,0:T(8,128)(2,1)S(1)} copy-done((bf16[192,2048]{1,0:T(8,128)(2,1)S(1)}, bf16[192,2048]{1,0:T(8,128)(2,1)}, u32[]{:S(2)}) %copy-start.1) | copy-done | bytes 786456
  3.9 0.0 copy-start.2
  3.9 0.9 %copy-done.2 = bf16[32,2048]{1,0:T(8,128)(2,1)S(1)} copy-done((bf16[32,2048]{1,0:T(8,128)(2,1)S(1)}, bf16[32,2048]{1,0:T(8,128)(2,1)}, u32[]{:S(2)}) %copy-start.2) | copy-done | bytes 131096
  4.8 0.0 copy-start.3
  4.8 0.9 %copy-done.3 = bf16[256,256]{1,0:T(8,128)(2,1)S(1)} copy-done((bf16[256,256]{1,0:T(8,128)(2,1)S(1)}, bf16[256,256]{1,0:T(8,128)(2,1)}, u32[]{:S(2)}) %copy-start.3) | copy-done | bytes 131096
  5.7 0.0 copy-start.4
  5.7 0.9 %copy-done.4 = bf16[256,256]{1,0:T(8,128)(2,1)S(1)} copy-done((bf16[256,256]{1,0:T(8,128)(2,1)S(1)}, bf16[256,256]{1,0:T(8,128)(2,1)}, u32[]{:S(2)}) %copy-start.4) | copy-done | bytes 131096
  6.6 0.0 copy-start.5
  6.6 0.9 %copy-done.5 = bf16[256,256]{1,0:T(8,128)(2,1)S(1)} copy-done((bf16[256,256]{1,0:T(8,128)(2,1)S(1)}, bf16[256,256]{1,0:T(8,128)(2,1)}, u32[]{:S(2)}) %copy-start.5) | copy-done | bytes 131096
  7.5 0.0 copy-start.6
  7.5 0.9 %copy-done.6 = bf16[256,256]{1,0:T(8,128)(2,1)S(1)} copy-done((bf16[256,256]{1,0:T(8,128)(2,1)S(1)}, bf16[256,256]{1,0:T(8,128)(2,1)}, u32[]{:S(2)}) %copy-start.6) | copy-done | bytes 131096
  8.4 0.0 copy-start.7
  8.4 0.9 copy-done.7
  9.3 0.0 copy-start.8
  9.3 0.9 copy-done.8
  10.2 0.0 copy-start.9
  10.2 0.9 copy-done.9
  11.1 0.0 copy-start.10
  11.1 0.9 copy-done.10
  12.0 0.0 copy-start.11
  12.0 0.9 copy-done.11
  12.9 0.0 copy-start.12
  12.9 0.8 copy-done.12
  13.7 0.0 copy-start.13
  13.7 0.7 copy-done.13
  14.4 0.0 copy-start.14
  14.4 0.7 copy-done.14
  15.1 71.3 %shard_map.185 = (f32[1,192,2048]{2,1,0:T(8,128)S(1)}, f32[192,2048]{1,0:T(8,128)}) custom-call(bf16[128,8192]{1,0:T(8,128)(2,1)} %tok.1, bf16[192,2048]{1,0:T(8,128)(2,1)S(1)} %copy-done.1, bf16[128,192]{1,0:T(8,128)(2,1)S(1)} %copy.20.cot, f32[1,192,2048]{2,1,0:T(8,128)} %mom.1, s32[1,3,32,32]{3,2,1,0:T(8,128)S(1)} %copy-done.12, ...), custom_call_target="tpu_custom_call" | custom-call | tf_op jit(solution)/shard_map/pallas_call | solution.py:332
  86.4 0.0 copy-start.15
  86.4 1.1 %copy.23 = f32[1,192,2048]{2,1,0:T(8,128)} copy(f32[1,192,2048]{2,1,0:T(8,128)S(1)} %get-tuple-element.4) | data formatting | bytes 3145728
  87.6 0.8 copy-done.15
  88.4 1.1 %copy.24 = f32[192,2048]{1,0:T(8,128)} copy(f32[192,2048]{1,0:T(8,128)S(1)} %copy-done.15) | data formatting | bytes 3145728
Async XLA Ops:
  1.5 1.2 %copy-start = (bf16[8,128,512]{2,1,0:T(8,128)(2,1)S(1)}, bf16[8,128,512]{2,1,0:T(8,128)(2,1)}, u32[]{:S(2)}) copy-start(bf16[8,128,512]{2,1,0:T(8,128)(2,1)} %constant.38.clone.wide8) | copy-start | bytes 3145732
  2.8 1.1 %copy-start.1 = (bf16[192,2048]{1,0:T(8,128)(2,1)S(1)}, bf16[192,2048]{1,0:T(8,128)(2,1)}, u32[]{:S(2)}) copy-start(bf16[192,2048]{1,0:T(8,128)(2,1)} %weight.1) | copy-start | bytes 2359300
  3.9 0.9 %copy-start.2 = (bf16[32,2048]{1,0:T(8,128)(2,1)S(1)}, bf16[32,2048]{1,0:T(8,128)(2,1)}, u32[]{:S(2)}) copy-start(bf16[32,2048]{1,0:T(8,128)(2,1)} %constant.36.clone.wide) | copy-start | bytes 393220
  4.8 0.9 %copy-start.3 = (bf16[256,256]{1,0:T(8,128)(2,1)S(1)}, bf16[256,256]{1,0:T(8,128)(2,1)}, u32[]{:S(2)}) copy-start(bf16[256,256]{1,0:T(8,128)(2,1)} %constant.33.clone.inv_rl) | copy-start | bytes 393220
  5.7 0.9 %copy-start.4 = (bf16[256,256]{1,0:T(8,128)(2,1)S(1)}, bf16[256,256]{1,0:T(8,128)(2,1)}, u32[]{:S(2)}) copy-start(bf16[256,256]{1,0:T(8,128)(2,1)} %constant.32.clone.inv_rh) | copy-start | bytes 393220
  6.6 0.9 %copy-start.5 = (bf16[256,256]{1,0:T(8,128)(2,1)S(1)}, bf16[256,256]{1,0:T(8,128)(2,1)}, u32[]{:S(2)}) copy-start(bf16[256,256]{1,0:T(8,128)(2,1)} %constant.29.clone.fwd_rl) | copy-start | bytes 393220
  7.5 0.9 %copy-start.6 = (bf16[256,256]{1,0:T(8,128)(2,1)S(1)}, bf16[256,256]{1,0:T(8,128)(2,1)}, u32[]{:S(2)}) copy-start(bf16[256,256]{1,0:T(8,128)(2,1)} %constant.28.clone.fwd_rh) | copy-start | bytes 393220
  8.4 0.9 copy-start.7
  9.3 0.9 copy-start.8
  10.2 0.9 copy-start.9
  11.1 0.9 copy-start.10
  12.0 0.9 copy-start.11
  12.9 0.8 copy-start.12
  13.7 0.7 copy-start.13
  14.4 0.7 copy-start.14
  86.4 2.0 %copy-start.15 = (f32[192,2048]{1,0:T(8,128)S(1)}, f32[192,2048]{1,0:T(8,128)}, u32[]{:S(2)}) copy-start(f32[192,2048]{1,0:T(8,128)} %get-tuple-element.5) | copy-start | bytes 4718596

commit v2 on v1

--- a/solution.py
+++ b/solution.py
@@ -3,8 +3,6 @@
 
 import jax
 import jax.numpy as jnp
-import ml_dtypes
-import numpy as np
 from jax import lax
 from jax.experimental import pallas as pl
 from jax.experimental.pallas import tpu as pltpu
@@ -22,17 +20,32 @@
 MESH = pl.DeviceIdType.MESH
 
 
-def cosine_table():
-    n = np.arange(SPAN, dtype=np.float64)
-    angles = math.pi * (2.0 * n[None, :] + 1.0) * n[:, None] / (2.0 * SPAN)
-    scales = np.where(n[:, None] == 0, math.sqrt(1.0 / SPAN), math.sqrt(2.0 / SPAN))
-    return (scales * np.cos(angles)).astype(np.float32)
-
-
-def halves(table):
-    high = table.astype(ml_dtypes.bfloat16)
-    low = (table - high.astype(np.float32)).astype(ml_dtypes.bfloat16)
-    return high, low
+def iotas(shape):
+    return (
+        lax.broadcasted_iota(jnp.int32, shape, 0),
+        lax.broadcasted_iota(jnp.int32, shape, 1),
+    )
+
+
+def cosine_blocks(size, transposed):
+    row, col = iotas((size, size))
+    same = (row // SPAN) == (col // SPAN)
+    if transposed:
+        row, col = col, row
+    k, n = lax.rem(row, SPAN), lax.rem(col, SPAN)
+    turn = lax.rem((2 * n + 1) * k, 4 * SPAN)
+    turn = jnp.minimum(turn, 4 * SPAN - turn)
+    flip = turn > SPAN
+    turn = jnp.where(flip, 2 * SPAN - turn, turn)
+    angle = turn.astype(F32) * (math.pi / (2 * SPAN))
+    square = angle * angle
+    series = jnp.full_like(square, 1.0 / math.factorial(12))
+    for order in (10, 8, 6, 4, 2, 0):
+        sign = 1.0 if order % 4 == 0 else -1.0
+        series = series * square + sign / math.factorial(order)
+    series = jnp.where(flip, -series, series)
+    scale = jnp.where(k == 0, math.sqrt(1.0 / SPAN), math.sqrt(2.0 / SPAN))
+    return split(jnp.where(same, scale * series, 0.0))
 
 
 def split(x):
@@ -62,9 +75,9 @@
 def kernel(
     nf, nr,
     tok, weight, cot, mom, chosen,
-    fwd_lh, fwd_ll, fwd_rh, fwd_rl, inv_lh, inv_ll, inv_rh, inv_rl, eye, pair, wide, spot, wide8,
     new_out, upd_out,
     tok_v, w_own, wall, cot_v, mom_v, xall, gt, pos, delta, vt, new_v, upd_v,
+    fwd_lh, fwd_ll, fwd_rh, fwd_rl, inv_lh, inv_ll, inv_rh, inv_rl, eye, spot, wide8,
     s1_s, s1_r, s2_s, s2_r, s3_s, s3_r, x_s, x_r, g_s, g_r, p_s, p_r, v_s, v_r, loc, xloc, osem,
 ):
     r, f = lax.axis_index("replica"), lax.axis_index("fsdp")
@@ -130,6 +143,27 @@
         )
         sent_pos[t].start()
 
+    nbc = CHUNK // SPAN
+    for high_ref, low_ref, size, transposed in (
+        (fwd_lh, fwd_ll, rows, False),
+        (fwd_rh, fwd_rl, fwd_rh.shape[0], True),
+        (inv_lh, inv_ll, rows, True),
+        (inv_rh, inv_rl, fwd_rh.shape[0], False),
+    ):
+        high_ref[...], low_ref[...] = cosine_blocks(size, transposed)
+
+    def one_hot(equal):
+        return jnp.where(equal, 1.0, 0.0).astype(BF)
+
+    row, col = iotas((rows, rows))
+    eye[...] = one_hot(row == col)
+    row, col = iotas((2 * nbc, CHUNK))
+    spot[...] = one_hot(row == col // SPAN)
+    row, col = iotas((2 * GROUP * nbc, CHUNK))
+    near = lax.rem(row, GROUP * nbc) - col // SPAN
+    for i in range(GROUP):
+        wide8[i] = one_hot(near == i * nbc)
+
     xs = {}
 
     def send_x(c):
@@ -166,19 +200,23 @@
     c_pos.wait()
     for t in range(1, nr):
         sent_pos[t].wait_recv()
-    row = lax.broadcasted_iota(jnp.int32, (rows, CHUNK), 0)
-    col = lax.broadcasted_iota(jnp.int32, (rows, CHUNK), 1)
+    row, col = iotas((rows, CHUNK))
     target = (lax.rem(row, 2) * SPAN + lax.rem(col, SPAN)).astype(F32)
     run_start = lax.broadcasted_iota(jnp.int32, pos.shape[2:], 1) * RUN
+
+    row, col = iotas((SPAN, TOPK))
+    pair = one_hot(row // 2 == col)
+    row, col = iotas((dc // SPAN, CHUNK))
+    near = row - col // SPAN
 
     def locate(i, carry):
         parts = []
         for a in range(rows // SPAN):
             offset = (pos[i, a] - run_start).astype(F32).astype(BF)
-            parts.append(mm_nt(pair[...], offset))
+            parts.append(mm_nt(pair, offset))
         spots = jnp.concatenate(parts, axis=0).astype(BF)
         for c in range(nch):
-            far = mm(spots, wide[:, c * CHUNK : (c + 1) * CHUNK])
+            far = mm(spots, one_hot(near == c * nbc))
             delta[c, i] = (far - target).astype(BF)
         return carry
 
@@ -202,7 +240,7 @@
             pre = pre + mm_nt(wall[source, h], tok_v[:, cols])
 
     c_cot.wait()
-    up = mm_nt(eye[...], cot_v[...])
+    up = cot_v[...].astype(F32)
     s = jax.nn.sigmoid(pre)
     mine = pl.ds(pl.multiple_of(f * td, td), td)
     gt[:, mine] = (up * s * (1.0 + pre * (1.0 - s))).astype(BF)
@@ -238,7 +276,6 @@
         coef = transform(moment, fwd_lh[...], fwd_ll[...], fwd_rh[...], fwd_rl[...])
         own = jnp.where(delta[c, r].astype(F32) == 0.0, coef, 0.0)
         high, low = split(own)
-        nbc = CHUNK // SPAN
         vt[c, r] = (mm_nt(spot[...], high) + mm_nt(spot[...], low))[:nbc]
         for t in range(1, nr):
             sent_v[c, t] = remote(
@@ -256,7 +293,6 @@
         for t in range(1, nr):
             sent_v[c, t].wait_recv()
         cols = slice(c * CHUNK, (c + 1) * CHUNK)
-        nbc = CHUNK // SPAN
 
         def add_group(g, total):
             first = pl.multiple_of(g * GROUP, GROUP)
@@ -304,29 +340,9 @@
 def shards(nf, nr, tokens, weight, cotangent, momentum, chosen):
     td = tokens.shape[0]
     rows, dc = weight.shape
-    nb = dc // SPAN
     nch = dc // CHUNK
     nbc = CHUNK // SPAN
-    table = cosine_table()
-    left = np.kron(np.eye(rows // SPAN, dtype=np.float32), table)
-    right = np.kron(np.eye(4, dtype=np.float32), table)
-    fwd_lh, fwd_ll = halves(left)
-    fwd_rh, fwd_rl = halves(np.ascontiguousarray(right.T))
-    inv_lh, inv_ll = halves(np.ascontiguousarray(left.T))
-    inv_rh, inv_rl = halves(right)
-    bf = ml_dtypes.bfloat16
-    eye = np.eye(rows, dtype=np.float32).astype(bf)
-    pair = (np.arange(SPAN)[:, None] // 2 == np.arange(TOPK)[None, :]).astype(bf)
-    wide = (np.arange(dc)[None, :] // SPAN == np.arange(nb)[:, None]).astype(bf)
-    spot = (np.arange(CHUNK)[None, :] // SPAN == np.arange(2 * nbc)[:, None]).astype(bf)
-    slot = np.arange(2 * GROUP * nbc) % (GROUP * nbc)
-    wide8 = (
-        (slot[None, :, None] // nbc == np.arange(GROUP)[:, None, None])
-        & (slot[None, :, None] % nbc == np.arange(CHUNK)[None, None, :] // SPAN)
-    ).astype(bf)
-    consts = (
-        fwd_lh, fwd_ll, fwd_rh, fwd_rl, inv_lh, inv_ll, inv_rh, inv_rl, eye, pair, wide, spot, wide8
-    )
+    side = 4 * SPAN
     dma = pltpu.SemaphoreType.DMA
     vm = pltpu.VMEM
     new, update = pl.pallas_call(
@@ -335,14 +351,13 @@
             jax.ShapeDtypeStruct((1, rows, dc), F32),
             jax.ShapeDtypeStruct((rows, dc), F32),
         ),
-        in_specs=[pl.BlockSpec(memory_space=pl.ANY)] * 5
-        + [pl.BlockSpec(memory_space=pltpu.VMEM)] * len(consts),
+        in_specs=[pl.BlockSpec(memory_space=pltpu.HBM)] * 5,
         out_specs=(pl.BlockSpec(memory_space=pl.ANY), pl.BlockSpec(memory_space=pl.ANY)),
         scratch_shapes=[
             vm(tokens.shape, BF),
             vm(weight.shape, BF),
             vm((nf, 2, rows, dc // 2), BF),
-            vm(cotangent.shape, BF),
+            vm((rows, td), BF),
             vm((rows, dc), F32),
             vm((nch, nf * td, CHUNK), BF),
             vm((rows, nf * td), BF),
@@ -351,6 +366,9 @@
             vm((nch, nr, nbc, rows), F32),
             vm((rows, dc), F32),
             vm((rows, dc), F32),
+            vm((rows, rows), BF), vm((rows, rows), BF), vm((side, side), BF), vm((side, side), BF),
+            vm((rows, rows), BF), vm((rows, rows), BF), vm((side, side), BF), vm((side, side), BF),
+            vm((rows, rows), BF), vm((2 * nbc, CHUNK), BF), vm((GROUP, 2 * GROUP * nbc, CHUNK), BF),
             dma((nf,)), dma((nf,)),
             dma((nf, 4)), dma((nf, 4)),
             dma((nf,)), dma((nf,)),
@@ -361,9 +379,9 @@
             dma((5,)), dma((nch,)), dma((2, nch)),
         ],
         compiler_params=pltpu.CompilerParams(
-            collective_id=0, has_side_effects=True, vmem_limit_bytes=48 * 1024 * 1024
+            collective_id=0, has_side_effects=True, vmem_limit_bytes=60 * 1024 * 1024
         ),
-    )(tokens, weight, cotangent, momentum, chosen, *consts)
+    )(tokens, weight, cotangent.T, momentum, chosen)
     return new, update
 
 

time: 90.2 us -> 76.2 us (0.84)
  local copies, waits for them, and re-layouts: 17.6 us -> 3.97 us
    unnamed x35 -> x4, local copies, waits for them, and re-layouts: 17.6 us -> 3.97 us
where the time goes in v2:
time: 76.2 us; the launch traced here: 76 us
  Pallas kernels  71.4 us (94%)
  local copies, waits for them, and re-layouts  3.97 us (5%)
    pallas_call x1, Pallas kernels, shards(): pl.pallas_call(functools.partial(kernel, nf, nr), out_shape=(jax.ShapeDty...  71.4 us
    unnamed x4, local copies, waits for them, and re-layouts  3.97 us

profile of v2, /device:TPU:0, one launch (start us, length us, event | category | flops | bytes accessed | tf_op | source)
XLA Modules:
  0.0 76.0 jit_solution(17524357205237249210)
XLA Ops:
  0.6 71.4 %shard_map.68 = (f32[1,192,2048]{2,1,0:T(8,128)}, f32[192,2048]{1,0:T(8,128)}) custom-call(bf16[128,8192]{1,0:T(8,128)(2,1)} %tok.1, bf16[192,2048]{1,0:T(8,128)(2,1)} %weight.1, bf16[192,128]{1,0:T(8,128)(2,1)} %bitcast.1, f32[1,192,2048]{2,1,0:T(8,128)} %mom.1, s32[1,3,32,32]{3,2,1,0:T(8,128)} %chosen.1), custom_call_target="tpu_custom_call" | custom-call | tf_op jit(solution)/shard_map/pallas_call | solution.py:348
  72.0 0.0 copy-start
  72.0 2.8 %copy.9 = f32[1,192,2048]{2,1,0:T(8,128)} copy(f32[1,192,2048]{2,1,0:T(8,128)} %get-tuple-element.4) | data formatting | bytes 3145728
  74.8 0.0 copy-done
  74.9 1.1 %copy.10 = f32[192,2048]{1,0:T(8,128)} copy(f32[192,2048]{1,0:T(8,128)S(1)} %copy-done) | data formatting | bytes 3145728
Async XLA Ops:
  72.0 2.8 %copy-start = (f32[192,2048]{1,0:T(8,128)S(1)}, f32[192,2048]{1,0:T(8,128)}, u32[]{:S(2)}) copy-start(f32[192,2048]{1,0:T(8,128)} %get-tuple-element.5) | copy-start | bytes 4718596
